TPU v7x, 32 devices: a whole 2x2x4 slice. The times are simulated.
32 devices in a mesh: dp: 8 (over y, x, core), mp: 4 (over z).
Axes of the slice: x: 2, y: 2, z: 4, core: 2. Of those that a mesh axis runs over, the one named last changes fastest.
Arguments:
- inputs: bfloat16 [16384, 768], P(('dp', 'mp')), may hold values from -6 to 6
- first_values: bfloat16 [16384, 384], P('dp'), may hold values from -6 to 6
- seq_lens: int32 [8], P('dp'), may hold values from 64 to 2048, as said below
- attn_gain: float32 [768], replicated, may hold values from 0.1 to 1.9
- attn_shift: float32 [768], replicated, may hold values from -3 to 3
- query_weight: bfloat16 [768, 768], P(None, 'mp'), may hold values from -0.21875 to 0.21875
- query_bias: float32 [768], P('mp'), may hold values from -3 to 3
- key_weight: bfloat16 [768, 768], P(None, 'mp'), may hold values from -0.21875 to 0.21875
- value_weight: bfloat16 [768, 384], replicated, may hold values from -0.21875 to 0.21875
- value_bias: float32 [384], replicated, may hold values from -3 to 3
- out_weight: bfloat16 [768, 768], P('mp'), may hold values from -0.875 to 0.875
- out_bias: float32 [768], replicated, may hold values from -3 to 3
- mlp_gain: float32 [768], replicated, may hold values from 0.1 to 1.9
- mlp_shift: float32 [768], replicated, may hold values from -3 to 3
- expand_weight: bfloat16 [768, 3072], P(None, 'mp'), may hold values from -0.21875 to 0.21875
- expand_bias: float32 [3072], P('mp'), may hold values from -3 to 3
- contract_weight: bfloat16 [3072, 768], P('mp'), may hold values from -0.109375 to 0.109375
- contract_bias: float32 [768], replicated, may hold values from -3 to 3
- cotangent: bfloat16 [16384, 768], P('dp'), may hold values from -6 to 6
Outputs:
- layer_out: bfloat16 [16384, 768], P(('dp', 'mp'))
- grad_inputs: float32 [16384, 768], P(('dp', 'mp'))
- grad_first_values: float32 [16384, 384], P('dp', 'mp')
- grad_attn_gain: float32 [768], replicated
- grad_attn_shift: float32 [768], replicated
- grad_query_weight: float32 [768, 768], P(None, 'mp')
- grad_query_bias: float32 [768], P('mp')
- grad_key_weight: float32 [768, 768], P(None, 'mp')
- grad_value_weight: float32 [768, 384], replicated
- grad_value_bias: float32 [384], replicated
- grad_out_weight: float32 [768, 768], P('mp')
- grad_out_bias: float32 [768], replicated
- grad_mlp_gain: float32 [768], replicated
- grad_mlp_shift: float32 [768], replicated
- grad_expand_weight: float32 [768, 3072], P(None, 'mp')
- grad_expand_bias: float32 [3072], P('mp')
- grad_contract_weight: float32 [3072, 768], P('mp')
- grad_contract_bias: float32 [768], replicated
Inputs may be any that keep to these rules, and one draw needn't show every extreme that they name: `seq_lens`: each slot holds one sequence of that many positions followed by padding; in every draw one length is exactly 2048 and one is exactly 64.
All inputs are finite; a program needn't handle non-finite values.
Results may differ from a plain program's by a relative error of at most 0.015.
Values may be sent and summed in bfloat16 or wider, within the bound.
No kernel may reach another device: no remote copies, remote signals or barrier semaphores. Data moves between devices by JAX's collectives and lax.ppermute only.
A program may use at most 128 MiB of HBM per device.

v0:
```python
import jax
import jax.numpy as jnp
from jax import lax
from jax.sharding import PartitionSpec as P

HEAD_DIM = 64
SLOT_LEN = 2048
Q_BLOCK = 512


NORM_EPS = 1e-05
MASKED = -1e30


def layer_norm(values_in, gain, shift):
    centre = jnp.mean(values_in, axis=-1, keepdims=True)
    centred = values_in - centre
    spread = jnp.mean(centred * centred, axis=-1, keepdims=True)
    return centred * lax.rsqrt(spread + NORM_EPS) * gain + shift


def matmul(left, right):
    return jnp.dot(left, right, preferred_element_type=jnp.float32)


def inner_rows(left, right):
    return lax.dot_general(
        left, right, (((0,), (0,)), ((), ())), preferred_element_type=jnp.float32
    )


def inner_cols(left, right):
    return lax.dot_general(
        left, right, (((1,), (1,)), ((), ())), preferred_element_type=jnp.float32
    )


def block_scores(queries, key_rows, value_rows, seq_lens, block_index):
    head_count = queries.shape[1] // HEAD_DIM
    slot_number = block_index // (SLOT_LEN // Q_BLOCK)
    first_row = block_index * Q_BLOCK
    base_row = slot_number * SLOT_LEN
    query_block = lax.dynamic_slice_in_dim(queries, first_row, Q_BLOCK, 0).reshape(
        Q_BLOCK, head_count, HEAD_DIM
    )
    key_block = key_rows.reshape(SLOT_LEN, head_count, HEAD_DIM)
    value_block = value_rows.reshape(SLOT_LEN, head_count, HEAD_DIM)
    scores = jnp.einsum(
        "qhd,khd->hqk", query_block, key_block, preferred_element_type=jnp.float32
    ) * HEAD_DIM ** (-0.5)
    length = lax.dynamic_index_in_dim(seq_lens, slot_number, 0, keepdims=False)
    query_pos = first_row - base_row + jnp.arange(Q_BLOCK, dtype=jnp.int32)[:, None]
    key_pos = jnp.arange(SLOT_LEN, dtype=jnp.int32)[None, :]
    allowed = (key_pos <= query_pos) & (key_pos < length)
    scores = jnp.where(allowed[None], scores, MASKED)
    return (scores, allowed, query_block, key_block, value_block)


def attend_forward(queries, key_rows, value_rows, seq_lens):
    total_rows, head_cols = queries.shape

    def one_block(block_index):
        scores, allowed, query_block, key_block, value_block = block_scores(
            queries, key_rows, value_rows, seq_lens, block_index
        )
        row_max = jnp.max(scores, axis=-1, keepdims=True)
        weights = jnp.exp(scores - row_max)
        row_total = jnp.sum(weights, axis=-1, keepdims=True)
        probabilities = (weights / row_total).astype(jnp.bfloat16)
        mixture = jnp.einsum(
            "hqk,khd->qhd", probabilities, value_block, preferred_element_type=jnp.float32
        )
        return (
            mixture.reshape(Q_BLOCK, head_cols).astype(jnp.bfloat16),
            (row_max + jnp.log(row_total))[:, :, 0],
        )

    outputs, log_totals = lax.map(one_block, jnp.arange(total_rows // Q_BLOCK, dtype=jnp.int32))
    return (outputs.reshape(total_rows, head_cols), log_totals)


def attend_backward(queries, key_rows, value_rows, grad_heads, log_totals, seq_lens):
    total_rows, head_cols = queries.shape
    head_count = head_cols // HEAD_DIM
    per_slot = SLOT_LEN // Q_BLOCK
    scale_factor = HEAD_DIM ** (-0.5)

    def step(carry, inner):
        key_grad, value_grad = carry
        block_index = 0 + inner
        scores, allowed, query_block, key_block, value_block = block_scores(
            queries, key_rows, value_rows, seq_lens, block_index
        )
        grad_block = lax.dynamic_slice_in_dim(
            grad_heads, block_index * Q_BLOCK, Q_BLOCK, 0
        ).reshape(Q_BLOCK, head_count, HEAD_DIM)
        log_block = lax.dynamic_index_in_dim(log_totals, block_index, 0, keepdims=False)
        weights = jnp.where(allowed[None], jnp.exp(scores - log_block[:, :, None]), 0.0)
        value_grad = value_grad + jnp.einsum(
            "hqk,qhd->khd",
            weights.astype(jnp.bfloat16),
            grad_block,
            preferred_element_type=jnp.float32,
        )
        grad_probs = jnp.einsum(
            "qhd,khd->hqk", grad_block, value_block, preferred_element_type=jnp.float32
        )
        centre = jnp.sum(weights * grad_probs, axis=-1, keepdims=True)
        grad_scores = (weights * (grad_probs - centre)).astype(jnp.bfloat16)
        query_grad = (
            jnp.einsum("hqk,khd->qhd", grad_scores, key_block, preferred_element_type=jnp.float32)
            * scale_factor
        )
        key_grad = (
            key_grad
            + jnp.einsum(
                "hqk,qhd->khd", grad_scores, query_block, preferred_element_type=jnp.float32
            )
            * scale_factor
        )
        return ((key_grad, value_grad), query_grad.reshape(Q_BLOCK, head_cols).astype(jnp.bfloat16))

    zero_grad = jnp.zeros((SLOT_LEN, head_count, HEAD_DIM), jnp.float32)
    (key_grad, value_grad), query_grad = lax.scan(
        step, (zero_grad, zero_grad), jnp.arange(per_slot, dtype=jnp.int32)
    )
    query_parts = query_grad.reshape(SLOT_LEN, head_cols)
    key_parts = key_grad.reshape(SLOT_LEN, head_cols).astype(jnp.bfloat16)
    value_parts = value_grad.reshape(SLOT_LEN, head_cols).astype(jnp.bfloat16)
    return (query_parts, key_parts, value_parts)


def shards(
    inputs,
    first_values,
    seq_lens,
    attn_gain,
    attn_shift,
    query_weight,
    query_bias,
    key_weight,
    value_weight,
    value_bias,
    out_weight,
    out_bias,
    mlp_gain,
    mlp_shift,
    expand_weight,
    expand_bias,
    contract_weight,
    contract_bias,
    cotangent,
):
    group_size = lax.axis_size("mp")
    member = lax.axis_index("mp")
    share_rows = inputs.shape[0]
    group_rows = share_rows * group_size
    first_row = member * share_rows
    model_width = inputs.shape[1]
    head_cols = query_weight.shape[1]
    fresh_count = group_size // 2
    fresh_member = member < fresh_count
    value_start = member % fresh_count * head_cols
    residual = inputs.astype(jnp.float32)
    normed_one = layer_norm(residual, attn_gain, attn_shift).astype(jnp.bfloat16)
    full_one = lax.all_gather(normed_one, "mp", axis=0, tiled=True)
    queries = (matmul(full_one, query_weight) + query_bias).astype(jnp.bfloat16)
    key_rows = matmul(full_one, key_weight).astype(jnp.bfloat16)
    value_cols = lax.dynamic_slice_in_dim(value_weight, value_start, head_cols, 1)
    value_shift = lax.dynamic_slice_in_dim(value_bias, value_start, head_cols, 0)
    reused = lax.dynamic_slice_in_dim(first_values, value_start, head_cols, 1)
    value_rows = lax.cond(
        fresh_member,
        lambda: (matmul(full_one, value_cols) + value_shift).astype(jnp.bfloat16),
        lambda: reused,
    )
    heads_out, log_totals = attend_forward(queries, key_rows, value_rows, seq_lens)
    attention = (
        lax.psum_scatter(matmul(heads_out, out_weight), "mp", scatter_dimension=0, tiled=True)
        + out_bias
    )
    residual_two = residual + attention
    normed_two = layer_norm(residual_two, mlp_gain, mlp_shift).astype(jnp.bfloat16)
    full_two = lax.all_gather(normed_two, "mp", axis=0, tiled=True)
    hidden = jax.nn.gelu(matmul(full_two, expand_weight) + expand_bias).astype(jnp.bfloat16)
    branch_out = (
        lax.psum_scatter(
            matmul(hidden, contract_weight).astype(jnp.bfloat16),
            "mp",
            scatter_dimension=0,
            tiled=True,
        ).astype(jnp.float32)
        + contract_bias
    )
    layer_out = (residual_two + branch_out).astype(jnp.bfloat16)
    positions = jnp.arange(group_rows, dtype=jnp.int32) % SLOT_LEN
    valid = positions < jnp.repeat(seq_lens, SLOT_LEN, total_repeat_length=group_rows)
    grad_out = jnp.where(valid[:, None], cotangent, jnp.zeros_like(cotangent))
    grad_share = lax.dynamic_slice_in_dim(grad_out, first_row, share_rows, 0).astype(jnp.float32)
    pre_act = matmul(full_two, expand_weight) + expand_bias
    _, gelu_back = jax.vjp(jax.nn.gelu, pre_act)
    grad_pre = gelu_back(inner_cols(grad_out, contract_weight))[0].astype(jnp.bfloat16)
    grad_contract = inner_rows(hidden, grad_out)
    grad_contract_bias = jnp.sum(grad_share, axis=0)
    grad_expand = inner_rows(full_two, grad_pre)
    grad_expand_bias = jnp.sum(grad_pre.astype(jnp.float32), axis=0)
    grad_normed_two = lax.psum_scatter(
        inner_cols(grad_pre, expand_weight), "mp", scatter_dimension=0, tiled=True
    )
    _, norm_two_back = jax.vjp(layer_norm, residual_two, mlp_gain, mlp_shift)
    grad_resid_two, grad_mlp_gain, grad_mlp_shift = norm_two_back(grad_normed_two)
    grad_resid_two = grad_resid_two + grad_share
    grad_attn = grad_resid_two.astype(jnp.bfloat16)
    grad_out_bias = jnp.sum(grad_attn.astype(jnp.float32), axis=0)
    grad_full = lax.all_gather(grad_attn, "mp", axis=0, tiled=True)
    grad_heads = inner_cols(grad_full, out_weight).astype(jnp.bfloat16)
    grad_out_weight = inner_rows(heads_out, grad_full)
    grad_queries, grad_keys, grad_values = attend_backward(
        queries, key_rows, value_rows, grad_heads, log_totals, seq_lens
    )
    grad_query_weight = inner_rows(full_one, grad_queries)
    grad_query_bias = jnp.sum(grad_queries.astype(jnp.float32), axis=0)
    grad_key_weight = inner_rows(full_one, grad_keys)
    summed = inner_cols(grad_queries, query_weight) + inner_cols(grad_keys, key_weight)
    grad_normed_one = lax.psum_scatter(
        (
            summed
            + lax.cond(
                fresh_member,
                lambda: inner_cols(grad_values, value_cols),
                lambda: jnp.zeros((share_rows * lax.axis_size("mp"), model_width), jnp.float32),
            )
        ).astype(jnp.bfloat16),
        "mp",
        scatter_dimension=0,
        tiled=True,
    ).astype(jnp.float32)
    _, norm_one_back = jax.vjp(layer_norm, residual, attn_gain, attn_shift)
    grad_resid_one, grad_attn_gain, grad_attn_shift = norm_one_back(grad_normed_one)
    grad_inputs = grad_resid_two + grad_resid_one
    fresh_scale = jnp.where(fresh_member, 1.0, 0.0).astype(jnp.float32)
    own_weight = lax.cond(
        fresh_member,
        lambda: inner_rows(full_one, grad_values),
        lambda: jnp.zeros((model_width, head_cols), jnp.float32),
    )
    own_bias = jnp.sum(grad_values.astype(jnp.float32), axis=0) * fresh_scale
    grad_value_weight = lax.dynamic_update_slice_in_dim(
        jnp.zeros(value_weight.shape, jnp.float32), own_weight, value_start, 1
    )
    grad_value_bias = lax.dynamic_update_slice_in_dim(
        jnp.zeros(value_bias.shape, jnp.float32), own_bias, value_start, 0
    )
    reuse_term = grad_values.astype(jnp.float32) * (1.0 - fresh_scale)
    value_term = lax.dynamic_update_slice_in_dim(
        jnp.zeros(first_values.shape, jnp.float32), reuse_term, value_start, 1
    )
    grad_first_values = lax.psum_scatter(
        value_term.astype(jnp.bfloat16), "mp", scatter_dimension=1, tiled=True
    ).astype(jnp.float32)
    summed_sharded = lax.psum(
        (
            grad_query_weight,
            grad_query_bias,
            grad_key_weight,
            grad_out_weight,
            grad_expand,
            grad_expand_bias,
            grad_contract,
        ),
        "dp",
    )
    summed_shared = lax.psum(
        (
            grad_value_weight,
            grad_value_bias,
            grad_attn_gain,
            grad_attn_shift,
            grad_out_bias,
            grad_mlp_gain,
            grad_mlp_shift,
            grad_contract_bias,
        ),
        ("dp", "mp"),
    )
    return (
        layer_out,
        grad_inputs,
        grad_first_values,
        summed_shared[2],
        summed_shared[3],
        summed_sharded[0],
        summed_sharded[1],
        summed_sharded[2],
        summed_shared[0],
        summed_shared[1],
        summed_sharded[3],
        summed_shared[4],
        summed_shared[5],
        summed_shared[6],
        summed_sharded[4],
        summed_sharded[5],
        summed_sharded[6],
        summed_shared[7],
    )


def solution(mesh):
    return jax.shard_map(
        shards,
        mesh=mesh,
        in_specs=(
            P(("dp", "mp"), None),
            P("dp", None),
            P("dp"),
            P(),
            P(),
            P(None, "mp"),
            P("mp"),
            P(None, "mp"),
            P(),
            P(),
            P("mp", None),
            P(),
            P(),
            P(),
            P(None, "mp"),
            P("mp"),
            P("mp", None),
            P(),
            P("dp", None),
        ),
        out_specs=(
            P(("dp", "mp"), None),
            P(("dp", "mp"), None),
            P("dp", "mp"),
            P(),
            P(),
            P(None, "mp"),
            P("mp"),
            P(None, "mp"),
            P(),
            P(),
            P("mp", None),
            P(),
            P(),
            P(),
            P(None, "mp"),
            P("mp"),
            P("mp", None),
            P(),
        ),
        check_vma=False,
    )
```

profile of v0, /device:TPU:0, one launch (start us, length us, event | category | flops | bytes accessed | tf_op | source)
XLA Modules:
  0.0 1144.6 jit_solution(12766825280296881614)
XLA Ops:
  13.7 65.3 %all-gather.4.cloned.1.call-done = bf16[2048,768]{1,0:T(8,128)(2,1)} async-done(((bf16[512,768]{1,0:T(8,128)(2,1)}), bf16[2048,768]{1,0:T(8,128)(2,1)}) %all-gather.4.cloned.1.call-update) | async-done | bytes 3145744 | tf_op jit(solution)/shard_map/all_gather | solution.py:166
  87.7 104.0 %while.33 = (s32[]{:T(128)}, bf16[4,512,192]{1,2,0:T(8,128)(2,1)}, f32[4,3,512]{2,1,0:T(4,128)}, s32[4]{0:T(128)S(1)}, s32[1]{0:T(128)}, /*index=5*/bf16[2048,19...) while((s32[]{:T(128)}, bf16[4,512,192]{1,2,0:T(8,128)(2,1)}, ...), condition=%wide.region_7.8_spmd, body=%wide.region_4.7_spmd.sunk | while | flops 845251584 | bytes 44755344 | solution.py:78
  93.0 6.0 fusion.137
  99.0 6.8 fusion.138
  105.7 6.7 fusion.139
  125.0 6.8 fusion.138
  131.7 6.7 fusion.139
  151.0 6.8 fusion.138
  157.7 6.7 fusion.139
  177.0 6.8 fusion.138
  183.7 6.7 fusion.139
  199.2 109.0 %reduce-scatter.6.cloned.1.call-done = f32[512,768]{1,0:T(8,128)} async-done(((f32[2048,768]{1,0:T(8,128)}), f32[512,768]{1,0:T(8,128)}) %reduce-scatter.6.cloned.1.call-update) | async-done | bytes 1572880 | tf_op jit(solution)/shard_map/reduce_scatter | solution.py:179
  316.7 59.7 %all-gather.6.cloned.1.call-done = bf16[2048,768]{1,0:T(8,128)(2,1)} async-done(((bf16[512,768]{1,0:T(8,128)(2,1)}), bf16[2048,768]{1,0:T(8,128)(2,1)}) %all-gather.6.cloned.1.call-update) | async-done | bytes 3145744 | tf_op jit(solution)/shard_map/all_gather | solution.py:184
  381.6 8.4 convert_reduce_fusion
  396.3 6.3 convolution_convert_fusion
  402.6 103.2 %reduce-scatter.10.cloned.1.call-done = f32[512,768]{1,0:T(8,128)} async-done(((f32[2048,768]{1,0:T(8,128)}), f32[512,768]{1,0:T(8,128)}) %reduce-scatter.10.cloned.1.call-update) | async-done | bytes 1572880 | tf_op jit(solution)/shard_map/reduce_scatter | solution.py:207
  508.4 60.3 %reduce-scatter.8.cloned.1.call-done = bf16[512,768]{1,0:T(8,128)(2,1)} async-done(((bf16[2048,768]{1,0:T(8,128)(2,1)}), bf16[512,768]{1,0:T(8,128)(2,1)}) %reduce-scatter.8.cloned.1.call-update) | async-done | bytes 786448 | tf_op jit(solution)/shard_map/reduce_scatter | solution.py:187
  576.3 63.4 %all-gather.8.cloned.1.call-done = bf16[2048,768]{1,0:T(8,128)(2,1)} async-done(((bf16[512,768]{1,0:T(8,128)(2,1)}), bf16[2048,768]{1,0:T(8,128)(2,1)}) %all-gather.8.cloned.1.call-update) | async-done | bytes 3145744 | tf_op jit(solution)/shard_map/all_gather | solution.py:215
  644.7 134.9 %while.34 = (s32[]{:T(128)}, f32[2048,3,64]{0,2,1:T(8,128)S(1)}, f32[2048,3,64]{0,2,1:T(8,128)}, bf16[4,512,192]{1,2,0:T(8,128)(2,1)}, s32[4]{0:T(128)S(1)}, /*i...) while((s32[]{:T(128)}, f32[2048,3,64]{0,2,1:T(8,128)S(1)}, ...), condition=%wide.region_17.18_spmd.clone, body=%wide.region_15.17_spmd.clone.sunk | while | flops 2048984064 | bytes 119904784 | solution.py:124
  654.8 7.9 multiply_reduce_fusion.5
  668.3 6.0 fusion.153
  688.5 7.9 multiply_reduce_fusion.5
  702.0 6.0 fusion.153
  722.2 7.9 multiply_reduce_fusion.5
  735.7 6.0 fusion.153
  756.0 7.9 multiply_reduce_fusion.5
  795.6 7.1 fusion.60
  824.1 15.5 %all-reduce.1 = (f32[192]{0:T(256)}, f32[768]{0:T(1024)}) all-reduce(f32[192]{0:T(256)S(1)} %convert_reduce_fusion.6, f32[768]{0:T(1024)S(1)} %copy-done.43), channel_id=1, replica_groups=mesh['dp'=8,'mp'=4] {'dp'}, use_global_device_ids=true, to_apply=%region_30.31 | all-reduce | flops 960 | bytes 7680 | tf_op jit(solution)/shard_map/psum | solution.py:261
  841.5 37.7 %reduce-scatter.12.cloned.1.call-done = bf16[512,768]{1,0:T(8,128)(2,1)} async-done(((bf16[2048,768]{1,0:T(8,128)(2,1)}), bf16[512,768]{1,0:T(8,128)(2,1)}) %reduce-scatter.12.cloned.1.call-update) | async-done | bytes 786448 | tf_op jit(solution)/shard_map/reduce_scatter | solution.py:225
  886.2 41.3 %all-reduce = (f32[768]{0:T(1024)}, f32[768]{0:T(1024)}, f32[384]{0:T(512)}, f32[768]{0:T(1024)}, f32[768]{0:T(1024)}, /*index=5*/f32[768]{0:T(1024)}, f32[768]{0:T(1024)}) all-reduce(f32[768]{0:T(1024)S(1)} %get-tuple-element.392, f32[768]{0:T(1024)S(1)} %get-tuple-element.395, ...), channel_id=1, replica_groups=mesh['dp'=8,'mp'=4] {'dp','mp'}, use_global_device_ids=true, to_apply=%region_25.26 | all-reduce | flops 4992 | bytes 39936 | tf_op jit(solution)/shard_map/psum | solution.py:273
  927.5 88.9 %all-reduce.6.cloned.1.call-done = f32[768,384]{1,0:T(8,128)} async-done(((f32[768,384]{1,0:T(8,128)}), f32[768,384]{1,0:T(8,128)}) %all-reduce.6.cloned.1.call-update) | async-done | bytes 1179664 | tf_op jit(solution)/shard_map/psum | solution.py:273
  1016.4 112.3 %all-reduce.8.cloned.1.call-done = (f32[768,192]{0,1:T(8,128)}, f32[768,192]{0,1:T(8,128)}, f32[192,768]{1,0:T(8,128)}, f32[768,768]{1,0:T(8,128)}, f32[768,768]{1,0:T(8,128)}) async-done(((f32[768,192]{0,1:T(8,128)}, f32[768,192]{0,1:T(8,128)}, f32[192,768]{1,0:T(8,128)}, f32[768,768]{1,0:T(8,128)}, f32[768,768]{1,0:T(8,128)}), (f32[768,192]{0,1:T(8,128)}, f32[768,192]{0,1:T(8,128)}, f32[192,768]{1,0:T(8,128)}, ...) | async-done | bytes 6488080 | tf_op jit(solution)/shard_map/psum | solution.py:261
  (282 shorter events, 217.9 us)
Async XLA Ops:
  7.2 374.3 %copy-start = (bf16[768,768]{1,0:T(8,128)(2,1)S(1)}, bf16[768,768]{1,0:T(8,128)(2,1)}, u32[]{:S(2)}) copy-start(bf16[768,768]{1,0:T(8,128)(2,1)} %param.49) | copy-start | bytes 3538948
  7.2 71.8 %copy-start.45 = (f32[384]{0:T(512)S(1)}, f32[384]{0:T(512)}, u32[]{:S(2)}) copy-start(f32[384]{0:T(512)} %param.42) | copy-start | bytes 4612
  7.2 71.8 %all-gather.4.cloned.1.call-start = ((), (), s32[]{:S(2)}) async-start(), calls=%async_computation.5 | async-start | bytes 3932160 | tf_op jit(solution)/shard_map/all_gather | solution.py:166
  8.7 70.3 %copy-start.29 = (f32[512]{0:T(512)}, f32[512]{0:T(512)S(1)}, u32[]{:S(2)}) copy-start(f32[512]{0:T(512)S(1)} %broadcast_multiply_fusion.2) | copy-start | bytes 6148
  10.2 68.8 %copy-start.37 = (f32[512]{0:T(512)}, f32[512]{0:T(512)S(1)}, u32[]{:S(2)}) copy-start(f32[512]{0:T(512)S(1)} %fusion.36) | copy-start | bytes 6148
  10.2 68.8 %copy-start.33 = (f32[512]{0:T(512)}, f32[512]{0:T(512)S(1)}, u32[]{:S(2)}) copy-start(f32[512]{0:T(512)S(1)} %fusion.45) | copy-start | bytes 6148
  12.7 295.5 %reduce-scatter.6.cloned.1.call-start = ((), (), s32[]{:S(2)}) async-start(), calls=%async_computation.6 | async-start | bytes 7864320 | tf_op jit(solution)/shard_map/reduce_scatter | solution.py:179
  191.7 7.4 copy-start.6
  191.7 7.4 copy-start.19
  199.1 109.1 %copy-start.44 = (f32[768]{0:T(1024)S(1)}, f32[768]{0:T(1024)}, u32[]{:S(2)}) copy-start(f32[768]{0:T(1024)} %param.44) | copy-start | bytes 9220
  199.1 111.3 %copy-start.32 = (f32[768]{0:T(1024)S(1)}, f32[768]{0:T(1024)}, u32[]{:S(2)}) copy-start(f32[768]{0:T(1024)} %param.45) | copy-start | bytes 9220
  199.1 177.3 %all-gather.6.cloned.1.call-start = ((), (), s32[]{:S(2)}) async-start(), calls=%async_computation.7 | async-start | bytes 3932160 | tf_op jit(solution)/shard_map/all_gather | solution.py:184
  312.3 193.5 %reduce-scatter.10.cloned.1.call-start = ((), (), s32[]{:S(2)}) async-start(), calls=%async_computation.9 | async-start | bytes 7864320 | tf_op jit(solution)/shard_map/reduce_scatter | solution.py:207
  381.6 10.1 copy-start.47
  396.2 172.5 %reduce-scatter.8.cloned.1.call-start = ((), (), s32[]{:S(2)}) async-start(), calls=%async_computation.8 | async-start | bytes 3932160 | tf_op jit(solution)/shard_map/reduce_scatter | solution.py:187
  402.6 166.2 %copy-start.42 = (f32[768]{0:T(1024)S(1)}, f32[768]{0:T(1024)}, u32[]{:S(2)}) copy-start(f32[768]{0:T(1024)} %param.50) | copy-start | bytes 9220
  402.6 237.2 %all-gather.8.cloned.1.call-start = ((), (), s32[]{:S(2)}) async-start(), calls=%async_computation.10 | async-start | bytes 3932160 | tf_op jit(solution)/shard_map/all_gather | solution.py:215
  572.0 71.7 %copy-start.35 = (f32[512]{0:T(512)}, f32[512]{0:T(512)S(1)}, u32[]{:S(2)}) copy-start(f32[512]{0:T(512)S(1)} %negate_multiply_fusion.1) | copy-start | bytes 6148
  576.0 263.5 %reduce-scatter.14.cloned.1.call-start = ((), (), s32[]{:S(2)}) async-start(), calls=%async_computation.12 | async-start | bytes 1966080 | tf_op jit(solution)/shard_map/reduce_scatter | solution.py:258
  576.3 68.4 %copy-start.7 = (bf16[2048,192]{0,1:T(8,128)(2,1)S(1)}, bf16[2048,192]{0,1:T(8,128)(2,1)}, u32[]{:S(2)}) copy-start(bf16[2048,192]{0,1:T(8,128)(2,1)} %copy-done.6) | copy-start | bytes 2359300
  783.5 95.7 %reduce-scatter.12.cloned.1.call-start = ((), (), s32[]{:S(2)}) async-start(), calls=%async_computation.11 | async-start | bytes 3932160 | tf_op jit(solution)/shard_map/reduce_scatter | solution.py:225
  795.6 220.8 %all-reduce.6.cloned.1.call-start = ((), (), s32[]{:S(2)}) async-start(), calls=%async_computation.13 | async-start | bytes 2359296 | tf_op jit(solution)/shard_map/psum | solution.py:273
  795.6 7.1 copy-start.46
  814.0 314.7 %all-reduce.8.cloned.1.call-start = ((), (), s32[]{:S(2)}) async-start(), calls=%async_computation.14 | async-start | bytes 12976128 | tf_op jit(solution)/shard_map/psum | solution.py:261
  822.8 56.4 %copy-start.4 = (bf16[512,768]{1,0:T(8,128)(2,1)S(1)}, bf16[512,768]{1,0:T(8,128)(2,1)}, u32[]{:S(2)}) copy-start(bf16[512,768]{1,0:T(8,128)(2,1)} %param.33) | copy-start | bytes 2359300
  822.8 56.4 %copy-start.30 = (f32[512]{0:T(512)S(1)}, f32[512]{0:T(512)}, u32[]{:S(2)}) copy-start(f32[512]{0:T(512)} %copy-done.29) | copy-start | bytes 6148
  822.8 56.4 %copy-start.31 = (f32[768]{0:T(1024)S(1)}, f32[768]{0:T(1024)}, u32[]{:S(2)}) copy-start(f32[768]{0:T(1024)} %param.36) | copy-start | bytes 9220
  822.8 58.1 %copy-start.38 = (f32[512]{0:T(512)S(1)}, f32[512]{0:T(512)}, u32[]{:S(2)}) copy-start(f32[512]{0:T(512)} %copy-done.37) | copy-start | bytes 6148
  822.8 58.1 %copy-start.34 = (f32[512]{0:T(512)S(1)}, f32[512]{0:T(512)}, u32[]{:S(2)}) copy-start(f32[512]{0:T(512)} %copy-done.33) | copy-start | bytes 6148
  822.8 60.3 %copy-start.9 = (f32[512,768]{1,0:T(8,128)S(1)}, f32[512,768]{1,0:T(8,128)}, u32[]{:S(2)}) copy-start(f32[512,768]{1,0:T(8,128)} %copy-done.8) | copy-start | bytes 4718596
  822.9 60.3 %copy-start.36 = (f32[512]{0:T(512)S(1)}, f32[512]{0:T(512)}, u32[]{:S(2)}) copy-start(f32[512]{0:T(512)} %copy-done.35) | copy-start | bytes 6148
  1016.4 116.3 %copy-start.23 = (f32[768,384]{1,0:T(8,128)S(1)}, f32[768,384]{1,0:T(8,128)}, u32[]{:S(2)}) copy-start(f32[768,384]{1,0:T(8,128)} %all-reduce.6.cloned.1.call-done) | copy-start | bytes 3538948
  (36 other events, 126.8 us)
Sparse Core Ops, SparseCore 0:
  12.8 66.1 all-gather.3
  199.2 108.8 reduce-scatter.5
  312.4 64.0 all-gather.5
  396.4 109.3 reduce-scatter.9
  507.9 60.7 reduce-scatter.7
  576.2 63.5 all-gather.7
  783.6 33.9 reduce-scatter.13
  819.9 59.2 reduce-scatter.11
  885.2 131.2 all-reduce.5
  1022.4 106.2 all-reduce.7
where the time goes:
time: 1150 us; the launch traced here: 1140 us
  waiting for transfers between devices  700 us (61%)
  matrix products  196 us (17%)
  other arithmetic  97.1 us (8%)
  blocking collectives  56.8 us (5%)
  local copies, waits for them, and re-layouts  45.7 us (4%)
  loops' own time  31.9 us (3%)
  between operations  15.8 us (1%)
    psum x1, waiting for transfers between devices, shards(): lax.psum((grad_query_weight, grad_query_bias, grad_key_weight, grad_out_w...  112 us
    reduce_scatter x1, waiting for transfers between devices, shards(): lax.psum_scatter(matmul(heads_out, out_weight), 'mp', scatter_dimension=0...  109 us
    reduce_scatter x1, waiting for transfers between devices, shards(): lax.psum_scatter(inner_cols(grad_pre, expand_weight), 'mp', scatter_dimen...  103 us
    psum x1, waiting for transfers between devices, shards(): lax.psum((grad_value_weight, grad_value_bias, grad_attn_gain, grad_attn_s...  88.9 us
    all_gather x1, waiting for transfers between devices, shards(): full_one = lax.all_gather(normed_one, 'mp', axis=0, tiled=True)  65.3 us
    all_gather x1, waiting for transfers between devices, shards(): grad_full = lax.all_gather(grad_attn, 'mp', axis=0, tiled=True)  63.4 us
    reduce_scatter x1, waiting for transfers between devices, shards(): lax.psum_scatter(matmul(hidden, contract_weight).astype(jnp.bfloat16), 'm...  60.3 us
    all_gather x1, waiting for transfers between devices, shards(): full_two = lax.all_gather(normed_two, 'mp', axis=0, tiled=True)  59.7 us
  transfers between devices with their start and end apart: 10, of which 9 were waited for; matrix products, arithmetic and copies ran while one was open for 5% of the time, Pallas kernels for 0%

commit v1 on v0

v1 whole, which is shorter than its diff:
```python
import functools
import math

import jax
import jax.numpy as jnp
from jax import lax
from jax.experimental import pallas as pl
from jax.experimental.pallas import tpu as pltpu
from jax.sharding import PartitionSpec as P

HEAD_DIM = 64
TILE = 512
K_TILE = 256
NORM_EPS = 1e-05
MASKED = -1e30
EMPTY = 1e30
LOG2_E = 1.4426950408889634
SCALE = HEAD_DIM ** (-0.5)
BF16 = jnp.bfloat16
F32 = jnp.float32
CHUNKS = ((0, 1, 2),)


def dot(left, right, left_dim, right_dim):
    return lax.dot_general(
        left, right, (((left_dim,), (right_dim,)), ((), ())), preferred_element_type=F32
    )


def two_parts(value):
    high = value.astype(BF16)
    return high, (value - high.astype(F32)).astype(BF16)


def three_rows(value, row):
    first = value.astype(BF16)
    rest = value - first.astype(F32)
    second = rest.astype(BF16)
    third = (rest - second.astype(F32)).astype(BF16)
    parts = [part.astype(F32) for part in (first, second, third)]
    empty = jnp.zeros(row.shape, F32)
    rows = jnp.where(row == 0, parts[0], jnp.where(row == 1, parts[1], jnp.where(row == 2, parts[2], empty)))
    return rows.astype(BF16)


def forward_kernel(length_ref, query_ref, key_ref, value_ref, out_ref, log_ref, keys, queries, values):
    slot = query_ref.shape[1]
    length = length_ref[0]
    row = lax.broadcasted_iota(jnp.int32, (16, slot), 0)
    position = lax.broadcasted_iota(jnp.int32, (16, slot), 1)
    first_row = jnp.where(row == 0, 1.0, 0.0).astype(BF16)
    padding = jnp.where((row == 0) & (position >= length), MASKED, 0.0).astype(BF16)
    high, low = two_parts(query_ref[...].astype(F32) * (SCALE * LOG2_E))
    queries[0:64] = high
    queries[64:128] = low
    queries[128:144] = first_row
    key_cols = key_ref[...]
    keys[...] = jnp.concatenate([key_cols, key_cols, padding], axis=0).T
    values[0:64] = value_ref[...]
    values[64:80] = first_row
    key_pos = lax.broadcasted_iota(jnp.int32, (TILE, TILE), 0)
    query_pos = lax.broadcasted_iota(jnp.int32, (TILE, TILE), 1)
    for block in range(slot // TILE):
        begin, end = block * TILE, (block + 1) * TILE
        scores = jnp.dot(keys[0:end, :], queries[:, begin:end], preferred_element_type=F32)
        corner = jnp.where(key_pos <= query_pos, scores[begin:], MASKED)
        top = jnp.max(corner, axis=0, keepdims=True)
        if block:
            top = jnp.maximum(top, jnp.max(scores[:begin], axis=0, keepdims=True))
        mixed = jnp.dot(
            values[:, begin:end], jnp.exp2(corner - top).astype(BF16), preferred_element_type=F32
        )
        if block:
            mixed = mixed + jnp.dot(
                values[:, 0:begin],
                jnp.exp2(scores[:begin] - top).astype(BF16),
                preferred_element_type=F32,
            )
        total = mixed[64:65]
        out_ref[:, begin:end] = (mixed[0:64] / total).astype(BF16)
        place = lax.broadcasted_iota(jnp.int32, (1, TILE), 1) + begin
        log_ref[:, begin:end] = jnp.where(place < length, top + jnp.log2(total), EMPTY)


def backward_kernel(
    query_ref, key_ref, value_ref, out_ref, grad_ref, log_ref,
    grad_query_ref, grad_key_ref, grad_value_ref,
    keys, queries, values, grads, query_rows, grad_rows, key_total, value_total,
):
    slot = query_ref.shape[1]
    row = lax.broadcasted_iota(jnp.int32, (16, slot), 0)
    ones = jnp.where(row < 3, 1.0, 0.0).astype(BF16)
    query_cols = query_ref[...]
    key_cols = key_ref[...]
    grad_cols = grad_ref[...]
    high, low = two_parts(query_cols.astype(F32) * (SCALE * LOG2_E))
    queries[0:64] = high
    queries[64:128] = low
    queries[128:144] = three_rows(-log_ref[...], row)
    keys[...] = jnp.concatenate([key_cols, key_cols, ones], axis=0).T
    values[...] = jnp.concatenate([value_ref[...], ones], axis=0).T
    centre = jnp.sum(grad_cols.astype(F32) * out_ref[...].astype(F32), axis=0, keepdims=True)
    grads[0:64] = grad_cols
    grads[64:80] = three_rows(-centre, row)
    query_rows[...] = query_cols.T
    grad_rows[...] = grad_cols.T
    key_total[...] = jnp.zeros_like(key_total)
    value_total[...] = jnp.zeros_like(value_total)
    for block in range(slot // TILE):
        begin, end = block * TILE, (block + 1) * TILE
        grad_query = jnp.zeros((HEAD_DIM, TILE), F32)
        for start in range(0, end, K_TILE):
            span = slice(start, start + K_TILE)
            scores = jnp.dot(keys[span, :], queries[:, begin:end], preferred_element_type=F32)
            shifted = jnp.dot(values[span, :], grads[:, begin:end], preferred_element_type=F32)
            weights = jnp.exp2(scores)
            if start >= begin:
                key_pos = lax.broadcasted_iota(jnp.int32, (K_TILE, TILE), 0) + start
                query_pos = lax.broadcasted_iota(jnp.int32, (K_TILE, TILE), 1) + begin
                weights = jnp.where(key_pos <= query_pos, weights, 0.0)
            grad_scores = (weights * shifted).astype(BF16)
            value_total[span, :] += jnp.dot(
                weights.astype(BF16), grad_rows[begin:end, :], preferred_element_type=F32
            )
            key_total[span, :] += jnp.dot(
                grad_scores, query_rows[begin:end, :], preferred_element_type=F32
            )
            grad_query = grad_query + jnp.dot(
                key_cols[:, span], grad_scores, preferred_element_type=F32
            )
        grad_query_ref[:, begin:end] = (grad_query * SCALE).astype(BF16)
    grad_key_ref[...] = (key_total[...].T * SCALE).astype(BF16)
    grad_value_ref[...] = value_total[...].T.astype(BF16)


VMEM_BYTES = 48 * 1024 * 1024


def attend_forward(queries, key_rows, value_rows, seq_lens, heads):
    slot = queries.shape[1]
    count, first = len(heads), heads[0]
    spec = pl.BlockSpec((HEAD_DIM, slot), lambda h: (h + first, 0))
    return pl.pallas_call(
        forward_kernel,
        grid=(count,),
        in_specs=[pl.BlockSpec(memory_space=pltpu.SMEM), spec, spec, spec],
        out_specs=[
            pl.BlockSpec((HEAD_DIM, slot), lambda h: (h, 0)),
            pl.BlockSpec((None, 1, slot), lambda h: (h, 0, 0)),
        ],
        out_shape=[
            jax.ShapeDtypeStruct((count * HEAD_DIM, slot), BF16),
            jax.ShapeDtypeStruct((count, 1, slot), F32),
        ],
        scratch_shapes=[
            pltpu.VMEM((slot, 144), BF16),
            pltpu.VMEM((144, slot), BF16),
            pltpu.VMEM((80, slot), BF16),
        ],
        compiler_params=pltpu.CompilerParams(vmem_limit_bytes=VMEM_BYTES),
        cost_estimate=pl.CostEstimate(
            flops=count * 8 * slot * slot * HEAD_DIM,
            bytes_accessed=count * slot * HEAD_DIM * 8,
            transcendentals=count * slot * slot // 2,
        ),
        name="attend_forward",
    )(seq_lens, queries, key_rows, value_rows)


def attend_backward(queries, key_rows, value_rows, outputs, grads, logs, heads):
    slot = queries.shape[1]
    count, first = len(heads), heads[0]
    whole = pl.BlockSpec((HEAD_DIM, slot), lambda h: (h + first, 0))
    part = pl.BlockSpec((HEAD_DIM, slot), lambda h: (h, 0))
    log_spec = pl.BlockSpec((None, 1, slot), lambda h: (h, 0, 0))
    return pl.pallas_call(
        backward_kernel,
        grid=(count,),
        in_specs=[whole, whole, whole, part, part, log_spec],
        out_specs=[part, part, part],
        out_shape=[jax.ShapeDtypeStruct((count * HEAD_DIM, slot), BF16)] * 3,
        scratch_shapes=[
            pltpu.VMEM((slot, 144), BF16),
            pltpu.VMEM((144, slot), BF16),
            pltpu.VMEM((slot, 80), BF16),
            pltpu.VMEM((80, slot), BF16),
            pltpu.VMEM((slot, HEAD_DIM), BF16),
            pltpu.VMEM((slot, HEAD_DIM), BF16),
            pltpu.VMEM((slot, HEAD_DIM), F32),
            pltpu.VMEM((slot, HEAD_DIM), F32),
        ],
        compiler_params=pltpu.CompilerParams(vmem_limit_bytes=VMEM_BYTES),
        cost_estimate=pl.CostEstimate(
            flops=count * 20 * slot * slot * HEAD_DIM,
            bytes_accessed=count * slot * HEAD_DIM * 16,
            transcendentals=count * slot * slot // 2,
        ),
        name="attend_backward",
    )(queries, key_rows, value_rows, outputs, grads, logs)


def normalize(values_in):
    centre = jnp.mean(values_in, axis=-1, keepdims=True)
    centred = values_in - centre
    spread = jnp.mean(centred * centred, axis=-1, keepdims=True)
    inverse = lax.rsqrt(spread + NORM_EPS)
    return centred * inverse, inverse


def normalize_back(normed, inverse, grads, gain):
    scaled = grads * gain
    mean_scaled = jnp.mean(scaled, axis=-1, keepdims=True)
    mean_product = jnp.mean(scaled * normed, axis=-1, keepdims=True)
    return inverse * (scaled - mean_scaled - normed * mean_product)


def gelu_parts(value):
    root = math.sqrt(2.0 / math.pi)
    bent = jnp.tanh(root * (value + 0.044715 * value * value * value))
    out = 0.5 * value * (1.0 + bent)
    slope = 0.5 * (1.0 + bent) + 0.5 * value * (1.0 - bent * bent) * root * (
        1.0 + 3 * 0.044715 * value * value
    )
    return out, slope


def line_gather(block, axis, size, member):
    rows = block.shape[0]
    up = down = block
    ups, downs = [], []
    for _ in range(size - 1):
        up = lax.ppermute(up, axis, [(i, i + 1) for i in range(size - 1)])
        down = lax.ppermute(down, axis, [(i + 1, i) for i in range(size - 1)])
        ups.append(up)
        downs.append(down)
    ordered = jnp.concatenate(ups[::-1] + [block] + downs, axis=0)
    return lax.dynamic_slice_in_dim(ordered, (size - 1 - member) * rows, size * rows, 0)


def exchange(pieces, axis):
    return lax.all_to_all(pieces, axis, 0, 0)


def cube_bits(size):
    return [1 << bit for bit in range(size.bit_length() - 1)]


def cube_sum(value, axis, size):
    for bit in cube_bits(size):
        value = value + lax.ppermute(value, axis, [(i, i ^ bit) for i in range(size)])
    return value


def shift_sum(value, axis, size):
    total = value
    for shift in range(1, size):
        total = total + lax.ppermute(value, axis, [(i, (i + shift) % size) for i in range(size)])
    return total


def cube_scatter(value, axis, size, index):
    for bit in cube_bits(size)[::-1]:
        halves = value.reshape((2, value.shape[0] // 2) + value.shape[1:])
        side = (index // bit) % 2
        kept = lax.dynamic_index_in_dim(halves, side, 0, keepdims=False)
        given = lax.dynamic_index_in_dim(halves, 1 - side, 0, keepdims=False).astype(BF16)
        came = lax.ppermute(given, axis, [(i, i ^ bit) for i in range(size)])
        value = kept + came.astype(F32)
    return value


def cube_gather(value, axis, size, index):
    for bit in cube_bits(size):
        came = lax.ppermute(value, axis, [(i, i ^ bit) for i in range(size)])
        side = (index // bit) % 2
        value = jnp.where(
            side == 1, jnp.concatenate([came, value], 0), jnp.concatenate([value, came], 0)
        )
    return value


def shards(
    mp_size, dp_size,
    inputs, first_values, seq_lens, attn_gain, attn_shift, query_weight, query_bias, key_weight,
    value_weight, value_bias, out_weight, out_bias, mlp_gain, mlp_shift, expand_weight, expand_bias,
    contract_weight, contract_bias, cotangent,
):
    member = lax.axis_index("mp")
    group = lax.axis_index("dp")
    share_rows, width = inputs.shape
    slot = share_rows * mp_size
    head_cols = query_weight.shape[1]
    fresh_count = mp_size // 2
    fresh = member < fresh_count
    value_start = member % fresh_count * head_cols
    half_width = value_weight.shape[1]

    def gather_weight(shards_of):
        pieces = []
        for shard in shards_of:
            rows = shard.shape[0] // dp_size
            pieces.append(lax.dynamic_slice_in_dim(shard, group * rows, rows, 0))
        whole = lax.all_gather(jnp.concatenate(pieces), ("mp", "dp"), axis=0, tiled=False)
        parts, begin = [], 0
        for piece in pieces:
            rows = piece.shape[0]
            parts.append(whole[:, begin : begin + rows].reshape(-1, width))
            begin += rows
        return parts

    residual = inputs.astype(F32)
    plain_one, inverse_one = normalize(residual)
    normed_one = (plain_one * attn_gain + attn_shift).astype(BF16)
    bias_rows = three_rows(jnp.broadcast_to(expand_bias, (16, expand_bias.shape[0])), lax.broadcasted_iota(jnp.int32, (16, width), 0))
    gathered = line_gather(jnp.concatenate([normed_one, bias_rows]), "mp", mp_size, member)
    gathered = gathered.reshape(mp_size, share_rows + 16, width)
    full_one = gathered[:, :share_rows].reshape(slot, width)
    expand_shift = jnp.sum(gathered[:, share_rows : share_rows + 3].astype(F32), axis=1).reshape(-1)
    out_all, expand_all = gather_weight((out_weight, expand_weight.T))
    (contract_all,) = gather_weight((contract_weight,))
    query_all, key_all = gather_weight((query_weight.T, key_weight.T))

    value_cols = lax.dynamic_slice_in_dim(value_weight, value_start, head_cols, 1)
    value_offset = lax.dynamic_slice_in_dim(value_bias, value_start, head_cols, 0)
    reused = lax.dynamic_slice_in_dim(first_values, value_start, head_cols, 1).T
    joined = jnp.concatenate([query_weight, key_weight, value_cols], axis=1)
    offsets = jnp.concatenate([query_bias, jnp.zeros_like(query_bias), value_offset])
    projected = (dot(joined, full_one, 0, 1) + offsets[:, None]).astype(BF16)
    queries = projected[:head_cols]
    key_rows = projected[head_cols : 2 * head_cols]
    value_rows = jnp.where(fresh, projected[2 * head_cols :], reused)

    logs, outputs, arrived = [], [], []
    for heads in CHUNKS:
        out, log = attend_forward(queries, key_rows, value_rows, seq_lens, heads)
        outputs.append(out)
        logs.append(log)
        pieces = out.reshape(out.shape[0], mp_size, share_rows).transpose(1, 0, 2)
        arrived.append(exchange(pieces, "mp"))
    heads_out = jnp.concatenate(arrived, axis=1).reshape(width, share_rows)

    residual_two = residual + dot(heads_out, out_all, 0, 0) + out_bias
    plain_two, inverse_two = normalize(residual_two)
    normed_two = (plain_two * mlp_gain + mlp_shift).astype(BF16)
    pre_act = dot(normed_two, expand_all, 1, 1) + expand_shift
    hidden, slope = gelu_parts(pre_act)
    hidden = hidden.astype(BF16)
    layer_out = (residual_two + dot(hidden, contract_all, 1, 0) + contract_bias).astype(BF16)

    places = member * share_rows + jnp.arange(share_rows, dtype=jnp.int32)
    own_cotangent = lax.dynamic_slice_in_dim(cotangent, member * share_rows, share_rows, 0)
    grad_out = jnp.where((places < seq_lens[0])[:, None], own_cotangent, jnp.zeros_like(own_cotangent))
    grad_pre = (dot(grad_out, contract_all, 1, 1) * slope).astype(BF16)

    def sum_weight(grad):
        rows = grad.shape[0] // (mp_size * dp_size)
        pieces = grad.astype(BF16).reshape(mp_size, dp_size, rows, width)
        pieces = lax.psum_scatter(pieces, "dp", scatter_dimension=1, tiled=False)
        piece = lax.psum_scatter(pieces, "mp", scatter_dimension=0, tiled=False)
        return lax.all_gather(piece, "dp", axis=0, tiled=True).astype(F32)

    grad_contract = sum_weight(dot(hidden, grad_out, 0, 0))
    grad_expand = sum_weight(dot(grad_pre, normed_two, 0, 0)).T
    grad_normed_two = dot(grad_pre, expand_all, 1, 0)
    grad_resid_two = grad_out.astype(F32) + normalize_back(plain_two, inverse_two, grad_normed_two, mlp_gain)
    grad_attn = grad_resid_two.astype(BF16)
    grad_out_weight = sum_weight(dot(heads_out, grad_attn, 1, 0))
    early = jnp.concatenate(
        [
            jnp.sum(grad_normed_two * plain_two, axis=0),
            jnp.sum(grad_normed_two, axis=0),
            jnp.sum(grad_attn.astype(F32), axis=0),
            jnp.sum(grad_out.astype(F32), axis=0),
            jnp.sum(grad_pre.astype(F32), axis=0),
        ]
    ).reshape(-1, width)
    early = shift_sum(cube_sum(early, "dp", dp_size), "mp", mp_size)

    grad_heads = dot(out_all, grad_attn, 1, 1).astype(BF16).reshape(mp_size, head_cols, share_rows)
    grads_back = []
    for heads, out, log in zip(CHUNKS, outputs, logs):
        rows = slice(heads[0] * HEAD_DIM, (heads[-1] + 1) * HEAD_DIM)
        came = exchange(grad_heads[:, rows], "mp")
        grad_full = came.transpose(1, 0, 2).reshape(-1, slot)
        grads_back.append(attend_backward(queries, key_rows, value_rows, out, grad_full, log, heads))

    returned = []
    for grads in grads_back:
        packed = jnp.stack([grads[0], grads[1], jnp.where(fresh, grads[2], jnp.zeros_like(grads[2]))])
        pieces = packed.reshape(3, -1, mp_size, share_rows).transpose(2, 0, 1, 3)
        returned.append(exchange(pieces, "mp"))
    grad_queries, grad_keys, grad_values = [
        jnp.concatenate([part[index] for part in grads_back], axis=0)
        for index in range(3)
    ]
    own = jnp.concatenate(returned, axis=2)
    own_queries = own[:, 0].reshape(width, share_rows)
    own_keys = own[:, 1].reshape(width, share_rows)
    own_values = own[:fresh_count, 2].reshape(half_width, share_rows)
    grad_normed_one = (
        dot(own_queries, query_all, 0, 0) + dot(own_keys, key_all, 0, 0) + dot(own_values, value_weight, 0, 1)
    )
    grad_inputs = grad_resid_two + normalize_back(plain_one, inverse_one, grad_normed_one, attn_gain)

    grad_joined = dot(jnp.concatenate([grad_queries, grad_keys, grad_values]), full_one, 1, 0)
    piece = cube_scatter(grad_joined.T, "dp", dp_size, group)
    own_value = piece[:, 2 * head_cols :] * jnp.where(fresh, 1.0, 0.0)
    value_piece = lax.dynamic_update_slice_in_dim(
        jnp.zeros((piece.shape[0], half_width), F32), own_value, value_start, 1
    )
    value_piece = shift_sum(value_piece.astype(BF16), "mp", mp_size)
    whole = cube_gather(
        jnp.concatenate([piece[:, : 2 * head_cols].astype(BF16), value_piece], axis=1), "dp", dp_size, group
    ).astype(F32)
    grad_query_weight = whole[:, :head_cols]
    grad_key_weight = whole[:, head_cols : 2 * head_cols]
    grad_value_weight = whole[:, 2 * head_cols :]

    out_cols = half_width // mp_size
    halves = grad_values.reshape(2, out_cols, slot)
    first_parts = [
        lax.ppermute(
            halves[part], "mp", [(fresh_count + i, 2 * i + part) for i in range(mp_size - fresh_count)]
        )
        for part in range(2)
    ]
    grad_first_values = jnp.where(member % 2 == 0, first_parts[0], first_parts[1]).astype(F32).T

    fresh_scale = jnp.where(fresh, 1.0, 0.0)
    query_sums = jnp.sum(grad_queries.astype(F32), axis=1)
    value_sums = jnp.sum(grad_values.astype(F32), axis=1) * fresh_scale
    late = jnp.concatenate(
        [
            jnp.sum(grad_normed_one * plain_one, axis=0),
            jnp.sum(grad_normed_one, axis=0),
            lax.dynamic_update_slice_in_dim(jnp.zeros((width,), F32), query_sums, member * head_cols, 0),
            lax.dynamic_update_slice_in_dim(jnp.zeros((width,), F32), value_sums, value_start, 0),
        ]
    ).reshape(-1, width)
    late = shift_sum(cube_sum(late, "dp", dp_size), "mp", mp_size)
    hidden_share = expand_bias.shape[0]
    return (
        layer_out,
        grad_inputs,
        grad_first_values,
        late[0],
        late[1],
        grad_query_weight,
        lax.dynamic_slice_in_dim(late[2], member * head_cols, head_cols, 0),
        grad_key_weight,
        grad_value_weight,
        late[3, :half_width],
        grad_out_weight,
        early[2],
        early[0],
        early[1],
        grad_expand,
        lax.dynamic_slice_in_dim(early[4:].reshape(-1), member * hidden_share, hidden_share, 0),
        grad_contract,
        early[3],
    )


def solution(mesh):
    rows, cols, both = P(("dp", "mp"), None), P(None, "mp"), P("mp", None)
    return jax.shard_map(
        functools.partial(shards, mesh.shape["mp"], mesh.shape["dp"]),
        mesh=mesh,
        in_specs=(
            rows, P("dp", None), P("dp"), P(), P(), cols, P("mp"), cols, P(), P(),
            both, P(), P(), P(), cols, P("mp"), both, P(), P("dp", None),
        ),
        out_specs=(
            rows, rows, P("dp", "mp"), P(), P(), cols, P("mp"), cols, P(), P(),
            both, P(), P(), P(), cols, P("mp"), both, P(),
        ),
        check_vma=False,
    )
```

time: 1150 us -> 520 us (0.45)
  waiting for transfers between devices: 700 us -> 238 us
  matrix products: 196 us -> 56.5 us
  other arithmetic: 97.1 us -> 23.6 us
  starting transfers between devices: 1.05 us -> 63 us
  blocking collectives: 56.8 us -> 9.63 us
  Pallas kernels: 0 us -> 32.2 us
  loops' own time: 31.9 us -> 0 us
  local copies, waits for them, and re-layouts: 45.7 us -> 72.3 us
    psum x2 -> x0, waiting for transfers between devices: 201 us -> none  [the longest x1 112 us: shards(): lax.psum((grad_query_weight, grad_query_bias, grad_key_weight, grad_out_w...]
    reduce_scatter x5 -> x6, waiting for transfers between devices: 310 us -> 110 us  [the longest x3 76.1 us: sum_weight(): pieces = lax.psum_scatter(pieces, 'dp', scatter_dimension=1, tiled=False)]
    all_gather x3 -> x5, waiting for transfers between devices: 188 us -> 33.8 us  [the longest x2 21.4 us: sum_weight(): return lax.all_gather(piece, 'dp', axis=0, tiled=True).astype(F32)]
    dot_general x45 -> x14, matrix products: 195 us -> 56.5 us  [dot(): lax.dot_general(left, right, (((left_dim,), (right_dim,)), ((), ())), pre...]
    ppermute x0 -> x29, waiting for transfers between devices: none -> 73.8 us  [the longest x3 56 us: line_gather(): up = lax.ppermute(up, axis, [(i, i + 1) for i in range(size - 1)])]
    psum x2 -> x0, blocking collectives: 56.8 us -> none  [the longest x1 41.3 us: shards(): lax.psum((grad_value_weight, grad_value_bias, grad_attn_gain, grad_attn_s...]
    ppermute x0 -> x29, starting transfers between devices: none -> 47.3 us  [the longest x3 18.3 us: line_gather(): up = lax.ppermute(up, axis, [(i, i + 1) for i in range(size - 1)])]
    reduce_sum x16 -> x7, other arithmetic: 49.5 us -> 4.25 us  [the longest x1 2.21 us: shards(): jnp.sum(grad_attn.astype(F32), axis=0)]
  transfers between devices with their start and end apart: 10 -> 43, of which waited for: 9 -> 19; matrix products, arithmetic and copies ran while one was open for 5% -> 27% of each run, Pallas kernels for 0% -> 6%
where the time goes in v1:
time: 520 us; the launch traced here: 511 us
  waiting for transfers between devices  238 us (46%)
  local copies, waits for them, and re-layouts  72.3 us (14%)
  starting transfers between devices  63 us (12%)
  matrix products  56.5 us (11%)
  Pallas kernels  32.2 us (6%)
  other arithmetic  23.6 us (5%)
  between operations  16.3 us (3%)
  blocking collectives  9.63 us (2%)
    reduce_scatter x3, waiting for transfers between devices, sum_weight(): pieces = lax.psum_scatter(pieces, 'dp', scatter_dimension=1, tiled=False)  76.1 us
    dot_general x14, matrix products, dot(): lax.dot_general(left, right, (((left_dim,), (right_dim,)), ((), ())), pre...  56.5 us
    ppermute x3, waiting for transfers between devices, line_gather(): up = lax.ppermute(up, axis, [(i, i + 1) for i in range(size - 1)])  56 us
    reduce_scatter x3, waiting for transfers between devices, sum_weight(): piece = lax.psum_scatter(pieces, 'mp', scatter_dimension=0, tiled=False)  33.5 us
    unnamed x114, local copies, waits for them, and re-layouts  26 us
    all_gather x2, waiting for transfers between devices, sum_weight(): return lax.all_gather(piece, 'dp', axis=0, tiled=True).astype(F32)  21.4 us
    pallas_call x1, Pallas kernels, attend_backward(): pl.pallas_call(backward_kernel, grid=(count,), in_specs=[whole, whole, wh...  21.4 us
    all_to_all x3, waiting for transfers between devices, exchange(): return lax.all_to_all(pieces, axis, 0, 0)  20.3 us
  transfers between devices with their start and end apart: 43, of which 19 were waited for; matrix products, arithmetic and copies ran while one was open for 27% of the time, Pallas kernels for 6%

profile of v1, /device:TPU:0, one launch (start us, length us, event | category | flops | bytes accessed | tf_op | source)
XLA Modules:
  0.0 511.0 jit_solution(41527708462786262)
XLA Ops:
  13.1 5.0 collective-permute-start
  19.4 19.9 %collective-permute-done = bf16[528,768]{1,0:T(8,128)(2,1)S(1)} collective-permute-done((bf16[528,768]{1,0:T(8,128)(2,1)S(1)}, bf16[528,768]{1,0:T(8,128)(2,1)S(1)}, u32[]{:S(2)}, u32[]{:S(2)}) %collective-permute-start) | collective-permute-done | bytes 811040 | tf_op jit(solution)/shard_map/ppermute | solution.py:232
  40.2 5.3 %collective-permute-start.1 = (bf16[528,768]{1,0:T(8,128)(2,1)S(1)}, bf16[528,768]{1,0:T(8,128)(2,1)}, u32[]{:S(2)}, u32[]{:S(2)}) collective-permute-start(bf16[528,768]{1,0:T(8,128)(2,1)S(1)} %collective-permute-done), channel_id=1, source_target_pairs={{0,1},{1,2},{2,3},{4,5},{5,6},{6,7},{8,9},{9,10},{10,11},{12,13},{... | collective-permute-start | bytes 2433032 | tf_op jit(solution)/shard_map/ppermute | solution.py:232
  46.7 25.3 %collective-permute-done.1 = bf16[528,768]{1,0:T(8,128)(2,1)} collective-permute-done((bf16[528,768]{1,0:T(8,128)(2,1)S(1)}, bf16[528,768]{1,0:T(8,128)(2,1)}, u32[]{:S(2)}, u32[]{:S(2)}) %collective-permute-start.1) | collective-permute-done | bytes 811040 | tf_op jit(solution)/shard_map/ppermute | solution.py:232
  72.0 8.0 %collective-permute-start.2 = (bf16[528,768]{1,0:T(8,128)(2,1)}, bf16[528,768]{1,0:T(8,128)(2,1)}, u32[]{:S(2)}, u32[]{:S(2)}) collective-permute-start(bf16[528,768]{1,0:T(8,128)(2,1)} %collective-permute-done.1), channel_id=1, source_target_pairs={{0,1},{1,2},{2,3},{4,5},{5,6},{6,7},{8,9},{9,10},{10,11},{12,13},{... | collective-permute-start | bytes 2433032 | tf_op jit(solution)/shard_map/ppermute | solution.py:232
  89.1 10.8 %collective-permute-done.2 = bf16[528,768]{1,0:T(8,128)(2,1)} collective-permute-done((bf16[528,768]{1,0:T(8,128)(2,1)}, bf16[528,768]{1,0:T(8,128)(2,1)}, u32[]{:S(2)}, u32[]{:S(2)}) %collective-permute-start.2) | collective-permute-done | bytes 811040 | tf_op jit(solution)/shard_map/ppermute | solution.py:232
  110.1 10.8 %attend_forward.1 = (bf16[192,2048]{1,0:T(8,128)(2,1)S(1)}, f32[3,1,2048]{2,1,0:T(1,128)S(1)}) custom-call(s32[1]{0:T(128)} %copy.110.length_ref, bf16[192,2048]{1,0:T(8,128)(2,1)S(1)} %get-tuple-element.107.query_ref, bf16[192,2048]{1,0:T(8,128)(2,1)S(1)} %get-tuple-element.106.key_ref, bf16[192,2048]{1,0:T(8,128)(2,1)S(1)} %get-tuple-element.105.value_ref), custom_call_target="tpu_custom_call" | custom-call | flops 6442450944 | bytes 3145728 | tf_op jit(solution)/shard_map/attend_forward/pallas_call | solution.py:143
  121.9 5.8 %all-to-all-start = ((bf16[4,192,512]{2,1,0:T(8,128)(2,1)}), bf16[4,192,512]{2,1,0:T(8,128)(2,1)S(1)}, u32[]{:S(2)}, u32[]{:S(2)}) async-start(bf16[4,192,512]{2,1,0:T(8,128)(2,1)} %bitcast.96), calls=%async_computation | async-start | bytes 1572864 | tf_op jit(solution)/shard_map/all_to_all | solution.py:241
  132.9 4.8 slice.120
  137.7 20.3 %all-to-all-done = bf16[4,192,512]{2,1,0:T(8,128)(2,1)S(1)} async-done(((bf16[4,192,512]{2,1,0:T(8,128)(2,1)}), bf16[4,192,512]{2,1,0:T(8,128)(2,1)S(1)}, u32[]{:S(2)}, u32[]{:S(2)}) %all-to-all-start) | async-done | bytes 786464 | tf_op jit(solution)/shard_map/all_to_all | solution.py:241
  161.9 4.8 fusion.42
  166.7 8.9 %convert_reduce_fusion = (f32[3072]{0:T(1024)S(1)}, bf16[512,3072]{1,0:T(8,128)(2,1)S(1)}) fusion(f32[512,3072]{1,0:T(8,128)} %fusion.42, f32[3072]{0:T(1024)S(1)} %add.264, bf16[3072,768]{1,0:T(8,128)(2,1)} %all-gather.14.cloned.1.call-done, bf16[2048,768]{1,0:T(8,128)(2,1)} %param.37, s32[]{:T(128)S(6)} %select_n.163, pred[512]{0:T(512)(128)(4,1)S(1)} %add_compare_fusion), kind=kOutput, calls=%fused_computation.9 | convolution fusion | flops 2450912256 | bytes 14967300 | tf_op jit(solution)/shard_map/dot_general | solution.py:25
  175.6 3.3 convolution_convert_fusion.1
  181.5 6.2 %multiply_reduce_fusion = (f32[768]{0:T(1024)S(1)}, f32[512]{0:T(512)S(1)}, f32[512]{0:T(512)S(1)}, f32[768]{0:T(1024)S(1)}, f32[512,768]{1,0:T(8,128)S(1)}) fusion(f32[512,768]{1,0:T(8,128)S(1)} %get-tuple-element.115, f32[512]{0:T(512)S(1)} %add_rsqrt_fusion, f32[512]{0:T(512)S(1)} %broadcast_multiply_fusion.4, f32[768]{0:T(1024)S(1)} %copy-done.37, ...), kind=kOutput, calls=%fused_computation.43 | convolution fusion | flops 2419455488 | bytes 11027456 | tf_op jit(solution)/shard_map/dot_general | solution.py:25
  192.2 6.5 %convolution_convert_fusion = bf16[3072,768]{1,0:T(8,128)(2,1)S(1)} fusion(bf16[2048,768]{1,0:T(8,128)(2,1)} %param.37, s32[]{:T(128)S(6)} %select_n.163, pred[512]{0:T(512)(128)(4,1)S(1)} %add_compare_fusion, f32[512,3072]{1,0:T(8,128)} %fusion.42, f32[3072]{0:T(1024)S(1)} %add.264), kind=kOutput, calls=%fused_computation.11 | convolution fusion | flops 2434400256 | bytes 11809284 | tf_op jit(solution)/shard_map/dot_general | solution.py:25
  201.4 4.8 copy.77
  209.3 3.5 all-to-all-start.1
  214.9 12.3 %all-gather.16.cloned.1.call-done = bf16[1536,768]{1,0:T(8,128)(2,1)} async-done(((bf16[48,768]{1,0:T(8,128)(2,1)}), bf16[1536,768]{1,0:T(8,128)(2,1)}) %all-gather.16.cloned.1.call-update) | async-done | bytes 2359312 | tf_op jit(solution)/shard_map/all_gather | solution.py:303
  227.2 3.3 fusion.44
  232.0 10.0 %add_convert_fusion.1 = bf16[512,768]{1,0:T(8,128)(2,1)} fusion(f32[512,768]{1,0:T(8,128)S(1)} %copy-done.15, bf16[3072,768]{1,0:T(8,128)(2,1)} %all-gather.14.cloned.1.call-done, f32[768]{0:T(1024)S(1)} %copy-done.47, f32[512,3072]{1,0:T(8,128)} %fusion.42, f32[3072]{0:T(1024)S(1)} %add.264), kind=kOutput, calls=%fused_computation.48 | convolution fusion | flops 2432827392 | bytes 13384704 | tf_op jit(solution)/shard_map/dot_general | solution.py:25
  248.6 21.4 %attend_backward.1 = (bf16[192,2048]{1,0:T(8,128)(2,1)S(1)}, bf16[192,2048]{1,0:T(8,128)(2,1)S(1)}, bf16[192,2048]{1,0:T(8,128)(2,1)S(1)}) custom-call(bf16[192,2048]{1,0:T(8,128)(2,1)S(1)} %copy-done.7, bf16[192,2048]{1,0:T(8,128)(2,1)S(1)} %copy-done.5, bf16[192,2048]{1,0:T(8,128)(2,1)S(1)} %copy-done.3, bf16[192,2048]{1,0:T(8,128)(2,1)S(1)} %get-tuple-element.23.out_ref, ...), custom_call_target="tpu_custom_call" | custom-call | flops 16106127360 | bytes 6291456 | tf_op jit(solution)/shard_map/attend_backward/pallas_call | solution.py:176
  273.0 3.9 fusion.7
  284.9 5.1 %all-to-all-start.2 = ((bf16[4,3,192,512]{3,2,1,0:T(8,128)(2,1)}), bf16[4,3,192,512]{3,2,1,0:T(8,128)(2,1)}, u32[]{:S(2)}, u32[]{:S(2)}) async-start(bf16[4,3,192,512]{3,2,1,0:T(8,128)(2,1)} %maximum_bitcast_fusion), calls=%async_computation.2 | async-start | bytes 4718592 | tf_op jit(solution)/shard_map/all_to_all | solution.py:241
  295.5 4.5 collective-permute-done.15
  300.8 23.5 %reduce-scatter.7.cloned.1.call-done = bf16[4,1,24,768]{3,2,0,1:T(8,128)(2,1)} async-done(((bf16[4,8,24,768]{3,2,0,1:T(8,128)(2,1)}), bf16[4,1,24,768]{3,2,0,1:T(8,128)(2,1)}) %reduce-scatter.7.cloned.1.call-update) | async-done | bytes 147472 | tf_op jit(solution)/shard_map/reduce_scatter | solution.py:358
  325.1 3.6 collective-permute-start.19
  329.6 51.9 %reduce-scatter.15.cloned.1.call-done = bf16[4,1,96,768]{3,2,0,1:T(8,128)(2,1)} async-done(((bf16[4,8,96,768]{3,2,0,1:T(8,128)(2,1)}), bf16[4,1,96,768]{3,2,0,1:T(8,128)(2,1)}) %reduce-scatter.15.cloned.1.call-update) | async-done | bytes 589840 | tf_op jit(solution)/shard_map/reduce_scatter | solution.py:358
  387.9 7.1 %collective-permute-done.21 = bf16[192,768]{1,0:T(8,128)(2,1)S(1)} collective-permute-done((bf16[192,768]{1,0:T(8,128)(2,1)S(1)}, bf16[192,768]{1,0:T(8,128)(2,1)S(1)}, u32[]{:S(2)}, u32[]{:S(2)}) %collective-permute-start.21) | collective-permute-done | bytes 294944 | tf_op jit(solution)/shard_map/ppermute | solution.py:274
  396.7 11.2 %reduce-scatter.13.cloned.1.call-done = bf16[1,96,768]{2,1,0:T(8,128)(2,1)} async-done(((bf16[4,96,768]{2,1,0:T(8,128)(2,1)}), bf16[1,96,768]{2,1,0:T(8,128)(2,1)}) %reduce-scatter.13.cloned.1.call-update) | async-done | bytes 147472 | tf_op jit(solution)/shard_map/reduce_scatter | solution.py:359
  408.9 19.5 %reduce-scatter.9.cloned.1.call-done = bf16[1,24,768]{2,1,0:T(8,128)(2,1)} async-done(((bf16[4,24,768]{2,1,0:T(8,128)(2,1)}), bf16[1,24,768]{2,1,0:T(8,128)(2,1)}) %reduce-scatter.9.cloned.1.call-update) | async-done | bytes 36880 | tf_op jit(solution)/shard_map/reduce_scatter | solution.py:359
  428.4 9.6 %all-gather.3 = bf16[1,192,768]{2,1,0:T(8,128)(2,1)S(1)} all-gather(bf16[1,24,768]{2,1,0:T(8,128)(2,1)} %reduce-scatter.9.cloned.1.call-done), channel_id=5, replica_groups=mesh['dp'=8,'mp'=4] {'dp'}, dimensions={1}, use_global_device_ids=true | all-gather | bytes 331776 | tf_op jit(solution)/shard_map/all_gather | solution.py:360
  481.2 20.0 %all-gather.20.cloned.1.call-done = bf16[1,768,768]{2,1,0:T(8,128)(2,1)} async-done(((bf16[1,96,768]{2,1,0:T(8,128)(2,1)}), bf16[1,768,768]{2,1,0:T(8,128)(2,1)}) %all-gather.20.cloned.1.call-update) | async-done | bytes 1179664 | tf_op jit(solution)/shard_map/all_gather | solution.py:360
  (303 shorter events, 133.7 us)
Async XLA Ops:
  7.3 123.3 %all-gather.12.cloned.1.call-start = ((), (), s32[]{:S(2)}) async-start(), calls=%async_computation.15 | async-start | bytes 6082560 | tf_op jit(solution)/shard_map/all_gather | solution.py:303
  10.2 156.5 %all-gather.14.cloned.1.call-start = ((), (), s32[]{:S(2)}) async-start(), calls=%async_computation.16 | async-start | bytes 4866048 | tf_op jit(solution)/shard_map/all_gather | solution.py:303
  13.1 26.2 %collective-permute-start = (bf16[528,768]{1,0:T(8,128)(2,1)S(1)}, bf16[528,768]{1,0:T(8,128)(2,1)S(1)}, u32[]{:S(2)}, u32[]{:S(2)}) collective-permute-start(bf16[528,768]{1,0:T(8,128)(2,1)S(1)} %pad_maximum_fusion), channel_id=1, source_target_pairs={{0,1},{1,2},{2,3},{4,5},{5,6},{6,7},{8,9},{9,10},{10,11},{12,13},{... | collective-permute-start | bytes 2433032 | tf_op jit(solution)/shard_map/ppermute | solution.py:232
  18.1 27.4 %collective-permute-start.3 = (bf16[528,768]{1,0:T(8,128)(2,1)S(1)}, bf16[528,768]{1,0:T(8,128)(2,1)}, u32[]{:S(2)}, u32[]{:S(2)}) collective-permute-start(bf16[528,768]{1,0:T(8,128)(2,1)S(1)} %pad_maximum_fusion), channel_id=1, source_target_pairs={{1,0},{2,1},{3,2},{5,4},{6,5},{7,6},{9,8},{10,9},{11,10},{13,12},{... | collective-permute-start | bytes 2433032 | tf_op jit(solution)/shard_map/ppermute | solution.py:233
  40.2 31.9 %collective-permute-start.1 = (bf16[528,768]{1,0:T(8,128)(2,1)S(1)}, bf16[528,768]{1,0:T(8,128)(2,1)}, u32[]{:S(2)}, u32[]{:S(2)}) collective-permute-start(bf16[528,768]{1,0:T(8,128)(2,1)S(1)} %collective-permute-done), channel_id=1, source_target_pairs={{0,1},{1,2},{2,3},{4,5},{5,6},{6,7},{8,9},{9,10},{10,11},{12,13},{... | collective-permute-start | bytes 2433032 | tf_op jit(solution)/shard_map/ppermute | solution.py:232
  45.5 42.2 %collective-permute-start.4 = (bf16[528,768]{1,0:T(8,128)(2,1)}, bf16[528,768]{1,0:T(8,128)(2,1)}, u32[]{:S(2)}, u32[]{:S(2)}) collective-permute-start(bf16[528,768]{1,0:T(8,128)(2,1)} %collective-permute-done.3), channel_id=1, source_target_pairs={{1,0},{2,1},{3,2},{5,4},{6,5},{7,6},{9,8},{10,9},{11,10},{13,12},{... | collective-permute-start | bytes 2433032 | tf_op jit(solution)/shard_map/ppermute | solution.py:233
  72.0 27.9 %collective-permute-start.2 = (bf16[528,768]{1,0:T(8,128)(2,1)}, bf16[528,768]{1,0:T(8,128)(2,1)}, u32[]{:S(2)}, u32[]{:S(2)}) collective-permute-start(bf16[528,768]{1,0:T(8,128)(2,1)} %collective-permute-done.1), channel_id=1, source_target_pairs={{0,1},{1,2},{2,3},{4,5},{5,6},{6,7},{8,9},{9,10},{10,11},{12,13},{... | collective-permute-start | bytes 2433032 | tf_op jit(solution)/shard_map/ppermute | solution.py:232
  87.7 17.9 %collective-permute-start.5 = (bf16[528,768]{1,0:T(8,128)(2,1)}, bf16[528,768]{1,0:T(8,128)(2,1)S(1)}, u32[]{:S(2)}, u32[]{:S(2)}) collective-permute-start(bf16[528,768]{1,0:T(8,128)(2,1)} %collective-permute-done.4), channel_id=1, source_target_pairs={{1,0},{2,1},{3,2},{5,4},{6,5},{7,6},{9,8},{10,9},{11,10},{13,12},{... | collective-permute-start | bytes 2433032 | tf_op jit(solution)/shard_map/ppermute | solution.py:233
  121.9 36.1 %all-to-all-start = ((bf16[4,192,512]{2,1,0:T(8,128)(2,1)}), bf16[4,192,512]{2,1,0:T(8,128)(2,1)S(1)}, u32[]{:S(2)}, u32[]{:S(2)}) async-start(bf16[4,192,512]{2,1,0:T(8,128)(2,1)} %bitcast.96), calls=%async_computation | async-start | bytes 1572864 | tf_op jit(solution)/shard_map/all_to_all | solution.py:241
  127.7 99.5 %all-gather.16.cloned.1.call-start = ((), (), s32[]{:S(2)}) async-start(), calls=%async_computation.17 | async-start | bytes 2433024 | tf_op jit(solution)/shard_map/all_gather | solution.py:303
  129.2 152.9 %reduce-scatter.11.cloned.1.call-start = ((), (), s32[]{:S(2)}) async-start(), calls=%async_computation.11 | async-start | bytes 5308416 | tf_op jit(solution)/shard_map/reduce_scatter | solution.py:358
  181.5 142.8 %reduce-scatter.7.cloned.1.call-start = ((), (), s32[]{:S(2)}) async-start(), calls=%async_computation.9 | async-start | bytes 1327104 | tf_op jit(solution)/shard_map/reduce_scatter | solution.py:358
  192.0 189.5 %reduce-scatter.15.cloned.1.call-start = ((), (), s32[]{:S(2)}) async-start(), calls=%async_computation.13 | async-start | bytes 5308416 | tf_op jit(solution)/shard_map/reduce_scatter | solution.py:358
  209.3 35.0 %all-to-all-start.1 = ((bf16[4,192,512]{2,1,0:T(8,128)(2,1)}), bf16[4,192,512]{2,1,0:T(8,128)(2,1)S(1)}, u32[]{:S(2)}, u32[]{:S(2)}) async-start(bf16[4,192,512]{2,1,0:T(8,128)(2,1)} %bitcast.124), calls=%async_computation.1 | async-start | bytes 1572864 | tf_op jit(solution)/shard_map/all_to_all | solution.py:241
  212.8 195.1 %reduce-scatter.13.cloned.1.call-start = ((), (), s32[]{:S(2)}) async-start(), calls=%async_computation.12 | async-start | bytes 737280 | tf_op jit(solution)/shard_map/reduce_scatter | solution.py:359
  212.9 17.7 %collective-permute-start.24 = (f32[8,768]{1,0:T(8,128)S(1)}, f32[8,768]{1,0:T(8,128)S(1)}, u32[]{:S(2)}, u32[]{:S(2)}) collective-permute-start(f32[8,768]{1,0:T(8,128)S(1)} %add.304), channel_id=1, source_target_pairs={{0,8},{4,12},{8,0},{12,4},{16,24},{20,28},{24,16},{28,20},{1,9},{5... | collective-permute-start | bytes 73736 | tf_op jit(solution)/shard_map/ppermute | solution.py:250
  242.0 52.8 %collective-permute-start.28 = (f32[8,768]{1,0:T(8,128)S(1)}, f32[8,768]{1,0:T(8,128)S(1)}, u32[]{:S(2)}, u32[]{:S(2)}) collective-permute-start(f32[8,768]{1,0:T(8,128)S(1)} %add.306), channel_id=1, source_target_pairs={{0,3},{1,0},{2,1},{3,2},{4,7},{5,4},{6,5},{7,6},{8,11},{9,8},{10,9... | collective-permute-start | bytes 73736 | tf_op jit(solution)/shard_map/ppermute | solution.py:257
  242.1 52.7 %collective-permute-start.27 = (f32[8,768]{1,0:T(8,128)S(1)}, f32[8,768]{1,0:T(8,128)S(1)}, u32[]{:S(2)}, u32[]{:S(2)}) collective-permute-start(f32[8,768]{1,0:T(8,128)S(1)} %add.306), channel_id=1, source_target_pairs={{0,2},{1,3},{2,0},{3,1},{4,6},{5,7},{6,4},{7,5},{8,10},{9,11},{10,... | collective-permute-start | bytes 73736 | tf_op jit(solution)/shard_map/ppermute | solution.py:257
  242.1 52.6 %collective-permute-start.26 = (f32[8,768]{1,0:T(8,128)S(1)}, f32[8,768]{1,0:T(8,128)S(1)}, u32[]{:S(2)}, u32[]{:S(2)}) collective-permute-start(f32[8,768]{1,0:T(8,128)S(1)} %add.306), channel_id=1, source_target_pairs={{0,1},{1,2},{2,3},{3,0},{4,5},{5,6},{6,7},{7,4},{8,9},{9,10},{10,1... | collective-permute-start | bytes 73736 | tf_op jit(solution)/shard_map/ppermute | solution.py:257
  277.8 12.3 %collective-permute-start.14 = (bf16[384,576]{0,1:T(8,128)(2,1)}, bf16[384,576]{0,1:T(8,128)(2,1)}, u32[]{:S(2)}, u32[]{:S(2)}) collective-permute-start(bf16[384,576]{0,1:T(8,128)(2,1)} %fusion.33), channel_id=1, source_target_pairs={{0,16},{4,20},{8,24},{12,28},{16,0},{20,4},{24,8},{28,12},{1,17},{... | collective-permute-start | bytes 1327112 | tf_op jit(solution)/shard_map/ppermute | solution.py:267
  284.9 155.5 %all-to-all-start.2 = ((bf16[4,3,192,512]{3,2,1,0:T(8,128)(2,1)}), bf16[4,3,192,512]{3,2,1,0:T(8,128)(2,1)}, u32[]{:S(2)}, u32[]{:S(2)}) async-start(bf16[4,3,192,512]{3,2,1,0:T(8,128)(2,1)} %maximum_bitcast_fusion), calls=%async_computation.2 | async-start | bytes 4718592 | tf_op jit(solution)/shard_map/all_to_all | solution.py:241
  290.0 138.4 %reduce-scatter.9.cloned.1.call-start = ((), (), s32[]{:S(2)}) async-start(), calls=%async_computation.10 | async-start | bytes 184320 | tf_op jit(solution)/shard_map/reduce_scatter | solution.py:359
  300.1 24.5 %collective-permute-start.16 = (bf16[96,576]{1,0:T(8,128)(2,1)S(1)}, bf16[96,576]{1,0:T(8,128)(2,1)S(1)}, u32[]{:S(2)}, u32[]{:S(2)}) collective-permute-start(bf16[96,576]{1,0:T(8,128)(2,1)S(1)} %fusion.35), channel_id=1, source_target_pairs={{0,4},{4,0},{8,12},{12,8},{16,20},{20,16},{24,28},{28,24},{1,5},{5... | collective-permute-start | bytes 331784 | tf_op jit(solution)/shard_map/ppermute | solution.py:267
  324.3 126.7 %reduce-scatter.17.cloned.1.call-start = ((), (), s32[]{:S(2)}) async-start(), calls=%async_computation.14 | async-start | bytes 737280 | tf_op jit(solution)/shard_map/reduce_scatter | solution.py:359
  325.1 59.3 %collective-permute-start.19 = (bf16[96,384]{1,0:T(8,128)(2,1)S(1)}, bf16[96,384]{1,0:T(8,128)(2,1)S(1)}, u32[]{:S(2)}, u32[]{:S(2)}) collective-permute-start(bf16[96,384]{1,0:T(8,128)(2,1)S(1)} %dynamic_update_slice.11), channel_id=1, source_target_pairs={{0,3},{1,0},{2,1},{3,2},{4,7},{5,4},{6,5},{7,6},{8,11},{9,8},{10,9... | collective-permute-start | bytes 221192 | tf_op jit(solution)/shard_map/ppermute | solution.py:257
  328.7 55.7 %collective-permute-start.18 = (bf16[96,384]{1,0:T(8,128)(2,1)S(1)}, bf16[96,384]{1,0:T(8,128)(2,1)S(1)}, u32[]{:S(2)}, u32[]{:S(2)}) collective-permute-start(bf16[96,384]{1,0:T(8,128)(2,1)S(1)} %dynamic_update_slice.11), channel_id=1, source_target_pairs={{0,2},{1,3},{2,0},{3,1},{4,6},{5,7},{6,4},{7,5},{8,10},{9,11},{10,... | collective-permute-start | bytes 221192 | tf_op jit(solution)/shard_map/ppermute | solution.py:257
  328.7 55.7 %collective-permute-start.17 = (bf16[96,384]{1,0:T(8,128)(2,1)S(1)}, bf16[96,384]{1,0:T(8,128)(2,1)S(1)}, u32[]{:S(2)}, u32[]{:S(2)}) collective-permute-start(bf16[96,384]{1,0:T(8,128)(2,1)S(1)} %dynamic_update_slice.11), channel_id=1, source_target_pairs={{0,1},{1,2},{2,3},{3,0},{4,5},{5,6},{6,7},{7,4},{8,9},{9,10},{10,1... | collective-permute-start | bytes 221192 | tf_op jit(solution)/shard_map/ppermute | solution.py:257
  381.5 93.6 %all-gather.18.cloned.1.call-start = ((), (), s32[]{:S(2)}) async-start(), calls=%async_computation.18 | async-start | bytes 1327104 | tf_op jit(solution)/shard_map/all_gather | solution.py:360
  382.4 25.6 %collective-permute-start.6 = (bf16[96,2048]{1,0:T(8,128)(2,1)}, bf16[96,2048]{1,0:T(8,128)(2,1)S(1)}, u32[]{:S(2)}, u32[]{:S(2)}) collective-permute-start(bf16[96,2048]{1,0:T(8,128)(2,1)} %get-tuple-element.109), channel_id=1, source_target_pairs={{2,0},{3,2},{6,4},{7,6},{10,8},{11,10},{14,12},{15,14},{18,16},{19... | collective-permute-start | bytes 1179656 | tf_op jit(solution)/shard_map/ppermute | solution.py:422
  383.7 24.3 %collective-permute-start.7 = (bf16[96,2048]{1,0:T(8,128)(2,1)S(1)}, bf16[96,2048]{1,0:T(8,128)(2,1)S(1)}, u32[]{:S(2)}, u32[]{:S(2)}) collective-permute-start(bf16[96,2048]{1,0:T(8,128)(2,1)S(1)} %get-tuple-element.108), channel_id=1, source_target_pairs={{2,1},{3,3},{6,5},{7,7},{10,9},{11,11},{14,13},{15,15},{18,17},{19... | collective-permute-start | bytes 1179656 | tf_op jit(solution)/shard_map/ppermute | solution.py:422
  395.3 43.7 %collective-permute-start.22 = (bf16[384,768]{1,0:T(8,128)(2,1)S(1)}, bf16[384,768]{1,0:T(8,128)(2,1)}, u32[]{:S(2)}, u32[]{:S(2)}) collective-permute-start(bf16[384,768]{1,0:T(8,128)(2,1)S(1)} %maximum_select_fusion.1), channel_id=1, source_target_pairs={{0,16},{4,20},{8,24},{12,28},{16,0},{20,4},{24,8},{28,12},{1,17},{... | collective-permute-start | bytes 1769480 | tf_op jit(solution)/shard_map/ppermute | solution.py:274
  407.9 93.2 %all-gather.20.cloned.1.call-start = ((), (), s32[]{:S(2)}) async-start(), calls=%async_computation.19 | async-start | bytes 1327104 | tf_op jit(solution)/shard_map/all_gather | solution.py:360
  (60 other events, 518.7 us)
Sparse Core Ops, SparseCore 0:
  11.6 77.4 all-gather.11
  92.5 70.9 all-gather.13
  166.9 60.2 all-gather.15
  230.5 51.5 reduce-scatter.10
  285.5 38.7 reduce-scatter.6
  327.6 53.8 reduce-scatter.14
  383.9 23.9 reduce-scatter.12
  410.2 18.1 reduce-scatter.8
  430.7 20.2 reduce-scatter.16
  452.8 22.3 all-gather.17
  477.1 24.0 all-gather.19
